TPU v7x, 32 devices: a whole 2x2x4 slice. The times are simulated.
32 devices in a mesh: noise: 4 (over y, x), row: 8 (over z, core).
Axes of the slice: x: 2, y: 2, z: 4, core: 2. Of those that a mesh axis runs over, the one named last changes fastest.
Arguments:
- activations: bfloat16 [16, 512, 768], P('noise', 'row'), may hold values from -6 to 6
- cond_scale: bfloat16 [16, 512, 768], P('noise', 'row'), may hold values from 0.25 to 16
- cond_shift: bfloat16 [16, 512, 768], P('noise', 'row'), may hold values from -4 to 4
- output_gate: bfloat16 [16, 512, 768], P('noise', 'row'), may hold values from -8 to 8
- pair_repr: bfloat16 [512, 512, 128], P('row', 'noise'), may hold values from -6 to 6
- bias_weight: bfloat16 [128, 8], replicated, may hold values from -1.5 to 1.5
- query_weight: bfloat16 [768, 384], P('noise'), may hold values from -0.21875 to 0.21875
- query_bias: bfloat16 [384], replicated, may hold values from -4 to 4
- key_weight: bfloat16 [768, 384], P('noise'), may hold values from -0.21875 to 0.21875
- value_weight: bfloat16 [768, 384], P('noise'), may hold values from -0.21875 to 0.21875
- output_weight: bfloat16 [384, 768], P('noise'), may hold values from -0.3125 to 0.3125
- token_mask: int32 [16, 512], P('noise', 'row'), may hold values from 0 to 1, as said below
Outputs:
- updated: bfloat16 [16, 512, 768], P('noise', 'row')
Inputs may be any that keep to these rules, and one draw needn't show every extreme that they name: `token_mask`: in each sample the tokens with mask 1 form a prefix of half of 512 tokens or more, and some sample has all 512 tokens.
All inputs are finite; a program needn't handle non-finite values.
Results may differ from a plain program's by a relative error of at most 0.012.
The roundings to bfloat16 on the way count: a program that leaves them out, or rounds other values in their place, can miss the bound.
Values may be sent and summed in bfloat16 or wider, within the bound.
No kernel may reach another device: no remote copies, remote signals or barrier semaphores. Data moves between devices by JAX's collectives and lax.ppermute only.
A program may use at most 128 MiB of HBM per device.

v0:
```python
import math

import jax
import jax.numpy as jnp
from jax import lax
from jax.sharding import PartitionSpec as P

epsilon = 1e-05
masked_score = -1e30


def layer_norm(tensor):
    average = jnp.mean(tensor, axis=-1, keepdims=True)
    centred = tensor - average
    variance = jnp.mean(centred * centred, axis=-1, keepdims=True)
    return centred * lax.rsqrt(variance + epsilon)


def body(
    activations,
    cond_scale,
    cond_shift,
    output_gate,
    pair_repr,
    bias_weight,
    query_weight,
    query_bias,
    key_weight,
    value_weight,
    output_weight,
    token_mask,
):
    samples_here, rows_here, features = activations.shape
    head_count = bias_weight.shape[1]
    head_features = query_weight.shape[1]
    head_width = head_features // head_count
    score_factor = 1.0 / math.sqrt(head_width)
    query_full, key_full, value_full, output_full = (
        lax.all_gather(query_weight, "noise", axis=0, tiled=True),
        lax.all_gather(key_weight, "noise", axis=0, tiled=True),
        lax.all_gather(value_weight, "noise", axis=0, tiled=True),
        lax.all_gather(output_weight, "noise", axis=0, tiled=True),
    )
    normed = layer_norm(activations.astype(jnp.float32))
    shifted = (cond_scale.astype(jnp.float32) * normed + cond_shift.astype(jnp.float32)).astype(
        jnp.bfloat16
    )
    flat_rows = shifted.reshape(samples_here * rows_here, features)
    queries = (
        jnp.dot(flat_rows, query_full, preferred_element_type=jnp.float32)
        + query_bias.astype(jnp.float32)
    ).astype(jnp.bfloat16)
    key_rows = jnp.dot(flat_rows, key_full, preferred_element_type=jnp.float32).astype(jnp.bfloat16)
    value_rows = jnp.dot(flat_rows, value_full, preferred_element_type=jnp.float32).astype(
        jnp.bfloat16
    )
    queries = queries.reshape(samples_here, rows_here, head_features)
    key_rows = key_rows.reshape(samples_here, rows_here, head_features)
    value_rows = value_rows.reshape(samples_here, rows_here, head_features)
    key_valid = token_mask.astype(jnp.bfloat16)
    pair_normed = layer_norm(pair_repr.astype(jnp.float32))
    bias_tile = jnp.einsum(
        "ijc,ch->hij", pair_normed, bias_weight.astype(jnp.float32), precision=lax.Precision.HIGHEST
    ).astype(jnp.bfloat16)
    bias_band = lax.all_gather(bias_tile, "noise", axis=2, tiled=True)
    query_heads = queries.reshape(samples_here, rows_here, head_count, head_width)
    running_max = jnp.full((samples_here, head_count, rows_here), -jnp.inf, jnp.float32)
    running_sum = jnp.zeros((samples_here, head_count, rows_here), jnp.float32)
    accumulated = jnp.zeros((samples_here, head_count, rows_here, head_width), jnp.float32)
    key_piece = lax.all_gather(key_rows, "row", axis=1, tiled=True)
    value_piece = lax.all_gather(value_rows, "row", axis=1, tiled=True)
    valid_piece = lax.all_gather(key_valid, "row", axis=1, tiled=True)
    piece_rows = key_piece.shape[1]
    key_heads = key_piece.reshape(samples_here, piece_rows, head_count, head_width)
    value_heads = value_piece.reshape(samples_here, piece_rows, head_count, head_width)
    bias_piece = bias_band.astype(jnp.float32)
    scores = (
        jnp.einsum("sihd,sjhd->shij", query_heads, key_heads, preferred_element_type=jnp.float32)
        * score_factor
        + bias_piece[None]
    )
    scores = jnp.where(valid_piece[:, None, None, :] > 0, scores, masked_score)
    updated_max = jnp.max(scores, axis=-1)
    factor = jnp.exp(running_max - updated_max)
    weights = jnp.exp(scores - updated_max[..., None])
    running_sum = running_sum * factor + jnp.sum(weights, axis=-1)
    accumulated = accumulated * factor[..., None] + jnp.einsum(
        "shij,sjhd->shid",
        weights.astype(jnp.bfloat16),
        value_heads,
        preferred_element_type=jnp.float32,
    )
    mixture = accumulated / running_sum[..., None]
    attended = (
        mixture.transpose(0, 2, 1, 3)
        .reshape(samples_here, rows_here, head_features)
        .astype(jnp.bfloat16)
    )
    projected = jnp.dot(
        attended.reshape(samples_here * rows_here, head_features),
        output_full,
        preferred_element_type=jnp.float32,
    ).reshape(samples_here, rows_here, features)
    return (
        activations.astype(jnp.float32)
        + jax.nn.sigmoid(output_gate.astype(jnp.float32)) * projected
    ).astype(jnp.bfloat16)


def solution(mesh):
    return jax.shard_map(
        body,
        mesh=mesh,
        in_specs=(
            P("noise", "row", None),
            P("noise", "row", None),
            P("noise", "row", None),
            P("noise", "row", None),
            P("row", "noise", None),
            P(),
            P("noise", None),
            P(),
            P("noise", None),
            P("noise", None),
            P("noise", None),
            P("noise", "row"),
        ),
        out_specs=P("noise", "row", None),
        check_vma=False,
    )
```

profile of v0, /device:TPU:0, one launch (start us, length us, event | category | flops | bytes accessed | tf_op | source)
XLA Modules:
  0.0 106.9 jit_solution(5520144606158595941)
XLA Ops:
  6.5 0.0 copy-start
  6.5 0.0 copy-start.5
  6.5 0.0 copy-start.2
  6.5 0.0 all-gather.4.cloned.1.call-start
  6.5 1.3 %convert_reduce_fusion.1 = f32[4,64]{1,0:T(4,128)S(1)} fusion(bf16[4,64,768]{2,1,0:T(8,128)(2,1)} %param.12), kind=kLoop, calls=%fused_computation.26 | loop fusion | flops 392960 | bytes 394240 | tf_op jit(solution)/shard_map/reduce_sum | solution.py:13
  7.8 1.2 %fusion.40 = f32[4,64]{1,0:T(4,128)S(1)} fusion(bf16[4,64,768]{2,1,0:T(8,128)(2,1)} %param.12, f32[4,64]{1,0:T(4,128)S(1)} %broadcast_multiply_fusion.1), kind=kLoop, calls=%fused_computation.36 | loop fusion | flops 786176 | bytes 395264 | tf_op jit(solution)/shard_map/reduce_sum | solution.py:15
  9.1 12.3 %all_gather.26 = bf16[768,384]{1,0:T(8,128)(2,1)S(1)} all-gather(bf16[192,384]{1,0:T(8,128)(2,1)} %param.20), channel_id=1, replica_groups=mesh['noise'=4,'row'=8] {'noise'}, dimensions={0}, use_global_device_ids=true | all-gather | bytes 737280 | tf_op jit(solution)/shard_map/all_gather | solution.py:40
  21.4 1.5 %fusion.43 = bf16[4,64,768]{2,1,0:T(8,128)(2,1)S(1)} fusion(bf16[4,64,768]{2,1,0:T(8,128)(2,1)} %param.12, bf16[4,64,768]{2,1,0:T(8,128)(2,1)} %param.14, bf16[4,64,768]{2,1,0:T(8,128)(2,1)} %param.13, f32[4,64]{1,0:T(4,128)S(1)} %add_rsqrt_fusion.1, f32[4,64]{1,0:T(4,128)S(1)} %broadcast_multiply_fusion.1), kind=kLoop, calls=%fused_computation.39 | loop fusion | flops 1572864 | bytes 1574912 | tf_op jit(solution)/shard_map/convert_element_type | solution.py:45
  22.9 1.1 convolution_convert_fusion.1
  24.0 0.0 all-gather.4.cloned.1.call-update
  24.0 0.0 all-gather.6.cloned.1.call-start
  24.0 0.0 copy-done.5
  24.0 10.4 %all_gather.29 = bf16[768,384]{1,0:T(8,128)(2,1)S(1)} all-gather(bf16[192,384]{1,0:T(8,128)(2,1)S(1)} %copy-done.5), channel_id=1, replica_groups=mesh['noise'=4,'row'=8] {'noise'}, dimensions={0}, use_global_device_ids=true | all-gather | bytes 737280 | tf_op jit(solution)/shard_map/all_gather | solution.py:41
  34.5 1.1 convolution_convert_fusion
  35.5 0.0 all-gather.6.cloned.1.call-update
  35.6 0.0 copy-done.2
  35.6 0.6 convert_reduce_fusion
  36.2 0.0 copy-start.9
  36.2 0.0 copy-start.6
  36.2 2.4 %fusion.2 = f32[64,128]{1,0:T(8,128)S(1)} fusion(bf16[64,128,128]{2,1,0:T(8,128)(2,1)S(1)} %copy-done.2, f32[64,128]{1,0:T(8,128)S(1)} %broadcast_multiply_fusion), kind=kLoop, calls=%fused_computation.4 | loop fusion | flops 4186112 | bytes 2162688 | tf_op jit(solution)/shard_map/reduce_sum | solution.py:15
  38.6 0.0 copy-start.8
  38.6 0.0 copy-start.7
  38.7 0.0 copy-done
  38.7 4.0 %fusion.29 = bf16[8,64,128]{2,0,1:T(8,128)(2,1)S(1)} fusion(bf16[64,128,128]{2,1,0:T(8,128)(2,1)S(1)} %copy-done.2, f32[64,128]{1,0:T(8,128)S(1)} %add_rsqrt_fusion, f32[64,128]{1,0:T(8,128)S(1)} %broadcast_multiply_fusion, bf16[128,8]{0,1:T(8,128)(2,1)S(1)} %copy-done), kind=kOutput, calls=%fused_computation.31 | convolution fusion | flops 103874560 | bytes 2295808 | tf_op jit(solution)/shard_map/ijc,ch->hij/dot_general | solution.py:62
  42.7 10.3 %all_gather.28 = bf16[8,64,512]{2,0,1:T(8,128)(2,1)S(1)} all-gather(bf16[8,64,128]{2,0,1:T(8,128)(2,1)S(1)} %fusion.29), channel_id=1, replica_groups=mesh['noise'=4,'row'=8] {'noise'}, dimensions={2}, use_global_device_ids=true | all-gather | bytes 655360 | tf_op jit(solution)/shard_map/all_gather | solution.py:65
  53.0 0.2 copy.29
  53.1 0.0 copy-done.9
  53.2 0.0 copy-done.6
  53.2 9.9 %all_gather.25 = bf16[768,384]{1,0:T(8,128)(2,1)S(1)} all-gather(bf16[192,384]{1,0:T(8,128)(2,1)S(1)} %copy-done.6), channel_id=1, replica_groups=mesh['noise'=4,'row'=8] {'noise'}, dimensions={0}, use_global_device_ids=true | all-gather | bytes 737280 | tf_op jit(solution)/shard_map/all_gather | solution.py:39
  63.1 0.4 fusion.25
  63.4 0.4 reshape.72
  63.9 0.0 copy-done.8
  63.9 12.1 %all-gather = bf16[8,64,4]{1,2,0:T(4,128)(2,1)S(1)} all-gather(bf16[1,64,4]{1,2,0:T(4,128)(2,1)S(1)} %convert_bitcast_fusion), channel_id=1, replica_groups=mesh['noise'=4,'row'=8] {'row'}, dimensions={0}, use_global_device_ids=true | all-gather | bytes 4608 | tf_op jit(solution)/shard_map/all_gather | solution.py:72
  76.0 0.1 reshape.69
  76.1 0.0 copy-done.7
  76.1 11.0 %all_gather.31 = bf16[384,768]{1,0:T(8,128)(2,1)} all-gather(bf16[96,768]{1,0:T(8,128)(2,1)S(1)} %copy-done.7), channel_id=1, replica_groups=mesh['noise'=4,'row'=8] {'noise'}, dimensions={0}, use_global_device_ids=true | all-gather | bytes 737280 | tf_op jit(solution)/shard_map/all_gather | solution.py:42
  87.1 0.0 all-gather.4.cloned.1.call-done
  87.1 1.7 %copy.27 = bf16[4,512,384]{1,2,0:T(8,128)(2,1)S(1)} copy(bf16[4,512,384]{2,1,0:T(8,128)(2,1)} %all-gather.4.cloned.1.call-done) | data formatting | bytes 3145728 | tf_op jit(solution)/shard_map/all_gather | solution.py:70
  88.8 0.9 fusion.7
  89.8 0.0 copy-start.1
  89.8 1.9 %copy-done.1 = f32[4,8,64,512]{3,2,1,0:T(8,128)} copy-done((f32[4,8,64,512]{3,2,1,0:T(8,128)}, f32[4,8,64,512]{3,2,1,0:T(8,128)S(1)}, u32[]{:S(2)}) %copy-start.1) | copy-done | bytes 4194328
  91.7 1.4 %fusion.5 = f32[4,8,64]{2,1,0:T(8,128)S(1)} fusion(f32[4,8,64,512]{3,2,1,0:T(8,128)S(1)} %get-tuple-element.6, f32[4,8,64]{2,1,0:T(8,128)S(1)} %get-tuple-element.5, f32[8,64,512]{2,1,0:T(8,128)S(1)} %copy.29, pred[4,512]{1,0:T(4,128)(4,1)S(1)} %bitcast.52), kind=kLoop, calls=%fused_computation.8 | loop fusion | flops 5240832 | bytes 5261312 | tf_op jit(solution)/shard_map/reduce_sum | solution.py:86
  93.2 0.0 all-gather.6.cloned.1.call-done
  93.2 1.7 %copy.30 = bf16[4,512,384]{1,2,0:T(8,128)(2,1)S(1)} copy(bf16[4,512,384]{2,1,0:T(8,128)(2,1)} %all-gather.6.cloned.1.call-done) | data formatting | bytes 3145728 | tf_op jit(solution)/shard_map/all_gather | solution.py:71
  94.9 0.0 copy-start.3
  94.9 0.0 copy-start.4
  94.9 0.0 copy-start.10
  94.9 3.9 %fusion.35 = bf16[4,64,8,48]{1,3,2,0:T(8,128)(2,1)S(1)} fusion(bf16[4,512,8,48]{1,3,2,0:T(8,128)(2,1)S(1)} %bitcast.48, f32[4,8,64,512]{3,2,1,0:T(8,128)} %copy-done.1, f32[4,8,64]{2,1,0:T(8,128)S(1)} %get-tuple-element.5, f32[8,64,512]{2,1,0:T(8,128)S(1)} %copy.29, pred[4,512]{1,0:T(4,128)(4,1)S(1)} %bitcast.53, f32[4,64,8]{1,2,0:T(8,128)S(1)} %bitcast_add_fusion, ...), kind=kOutput, calls=%fused_computation.33 | convolution fusion | flops 106201088 | bytes 7038976 | tf_op jit(solution)/shard_map/shij,sjhd->shid/dot_general | solution.py:87
  98.8 0.0 copy-done.3
  98.8 0.0 copy-done.4
  98.8 0.0 copy-done.10
  98.9 1.2 %fusion.24 = bf16[4,64,768]{2,1,0:T(8,128)(2,1)} fusion(bf16[4,64,384]{1,2,0:T(8,128)(2,1)S(1)} %bitcast.54, bf16[4,64,768]{2,1,0:T(8,128)(2,1)S(1)} %copy-done.3, bf16[4,64,768]{2,1,0:T(8,128)(2,1)S(1)} %copy-done.10, bf16[384,768]{1,0:T(8,128)(2,1)S(1)} %copy-done.4), kind=kOutput, calls=%fused_computation.23 | convolution fusion | flops 152567808 | bytes 1966080 | tf_op jit(solution)/shard_map/dot_general | solution.py:99
  (10 shorter events, 0.1 us)
Async XLA Ops:
  6.5 32.1 %copy-start = (bf16[128,8]{0,1:T(8,128)(2,1)S(1)}, bf16[128,8]{0,1:T(8,128)(2,1)}, u32[]{:S(2)}) copy-start(bf16[128,8]{0,1:T(8,128)(2,1)} %param.17) | copy-start | bytes 6148
  6.5 17.5 %copy-start.5 = (bf16[192,384]{1,0:T(8,128)(2,1)S(1)}, bf16[192,384]{1,0:T(8,128)(2,1)}, u32[]{:S(2)}) copy-start(bf16[192,384]{1,0:T(8,128)(2,1)} %param.21) | copy-start | bytes 442372
  6.5 29.0 %copy-start.2 = (bf16[64,128,128]{2,1,0:T(8,128)(2,1)S(1)}, bf16[64,128,128]{2,1,0:T(8,128)(2,1)}, u32[]{:S(2)}) copy-start(bf16[64,128,128]{2,1,0:T(8,128)(2,1)} %param.16) | copy-start | bytes 6291460
  6.5 80.6 %all-gather.4.cloned.1.call-start = ((), (), s32[]{:S(2)}) async-start(), calls=%async_computation | async-start | bytes 1769472 | tf_op jit(solution)/shard_map/all_gather | solution.py:70
  24.0 69.2 %all-gather.6.cloned.1.call-start = ((), (), s32[]{:S(2)}) async-start(), calls=%async_computation.1 | async-start | bytes 1769472 | tf_op jit(solution)/shard_map/all_gather | solution.py:71
  36.2 17.0 %copy-start.9 = (bf16[384]{0:T(512)(128)(2,1)S(1)}, bf16[384]{0:T(512)(128)(2,1)}, u32[]{:S(2)}) copy-start(bf16[384]{0:T(512)(128)(2,1)} %param.19) | copy-start | bytes 2308
  36.2 17.0 %copy-start.6 = (bf16[192,384]{1,0:T(8,128)(2,1)S(1)}, bf16[192,384]{1,0:T(8,128)(2,1)}, u32[]{:S(2)}) copy-start(bf16[192,384]{1,0:T(8,128)(2,1)} %param.18) | copy-start | bytes 442372
  38.6 25.3 %copy-start.8 = (s32[4,64]{1,0:T(4,128)S(1)}, s32[4,64]{1,0:T(4,128)}, u32[]{:S(2)}) copy-start(s32[4,64]{1,0:T(4,128)} %param.23) | copy-start | bytes 3076
  38.6 37.5 %copy-start.7 = (bf16[96,768]{1,0:T(8,128)(2,1)S(1)}, bf16[96,768]{1,0:T(8,128)(2,1)}, u32[]{:S(2)}) copy-start(bf16[96,768]{1,0:T(8,128)(2,1)} %param.22) | copy-start | bytes 442372
  89.8 1.9 %copy-start.1 = (f32[4,8,64,512]{3,2,1,0:T(8,128)}, f32[4,8,64,512]{3,2,1,0:T(8,128)S(1)}, u32[]{:S(2)}) copy-start(f32[4,8,64,512]{3,2,1,0:T(8,128)S(1)} %get-tuple-element.6) | copy-start | bytes 12582916
  94.9 3.9 %copy-start.3 = (bf16[4,64,768]{2,1,0:T(8,128)(2,1)S(1)}, bf16[4,64,768]{2,1,0:T(8,128)(2,1)}, u32[]{:S(2)}) copy-start(bf16[4,64,768]{2,1,0:T(8,128)(2,1)} %param.12) | copy-start | bytes 1179652
  94.9 3.9 %copy-start.4 = (bf16[384,768]{1,0:T(8,128)(2,1)S(1)}, bf16[384,768]{1,0:T(8,128)(2,1)}, u32[]{:S(2)}) copy-start(bf16[384,768]{1,0:T(8,128)(2,1)} %all_gather.31) | copy-start | bytes 1769476
  94.9 3.9 %copy-start.10 = (bf16[4,64,768]{2,1,0:T(8,128)(2,1)S(1)}, bf16[4,64,768]{2,1,0:T(8,128)(2,1)}, u32[]{:S(2)}) copy-start(bf16[4,64,768]{2,1,0:T(8,128)(2,1)} %param.15) | copy-start | bytes 1179652
Sparse Core Ops, SparseCore 0:
  24.1 25.3 all-gather.3
  51.1 24.3 all-gather.5
where the time goes:
time: 107 us
  blocking collectives  65.9 us (62%)
  between operations  13.7 us (13%)
  matrix products  12.5 us (12%)
  other arithmetic  8.57 us (8%)
  local copies, waits for them, and re-layouts  6.11 us (6%)
    all_gather x1, blocking collectives, body(): lax.all_gather(key_weight, 'noise', axis=0, tiled=True)  12.3 us
    all_gather x1, blocking collectives, body(): valid_piece = lax.all_gather(key_valid, 'row', axis=1, tiled=True)  12.1 us
    all_gather x1, blocking collectives, body(): lax.all_gather(output_weight, 'noise', axis=0, tiled=True)  11 us
    all_gather x1, blocking collectives, body(): lax.all_gather(value_weight, 'noise', axis=0, tiled=True)  10.4 us
    all_gather x1, blocking collectives, body(): bias_band = lax.all_gather(bias_tile, 'noise', axis=2, tiled=True)  10.3 us
    all_gather x1, blocking collectives, body(): lax.all_gather(query_weight, 'noise', axis=0, tiled=True)  9.89 us
    dot_general x1, matrix products, body(): jnp.einsum('ijc,ch->hij', pair_normed, bias_weight.astype(jnp.float32), p...  4.01 us
    dot_general x1, matrix products, body(): jnp.einsum('shij,sjhd->shid', weights.astype(jnp.bfloat16), value_heads,...  3.88 us
  transfers between devices with their start and end apart: 2, of which 0 were waited for; matrix products, arithmetic and copies ran while one was open for 12% of the time, Pallas kernels for 0%

commit v1 on v0

v1 whole, which is shorter than its diff:
```python
import functools
import math

import jax
import jax.numpy as jnp
from jax import lax
from jax.experimental import pallas as pl
from jax.experimental.pallas import tpu as pltpu
from jax.sharding import PartitionSpec as P

epsilon = 1e-05
masked_score = -1e30
absent = 32768.0
log2_e = math.log2(math.e)


def layer_norm(tensor):
    average = jnp.mean(tensor, axis=-1, keepdims=True)
    centred = tensor - average
    variance = jnp.mean(centred * centred, axis=-1, keepdims=True)
    return centred * lax.rsqrt(variance + epsilon)


def shift_kernel(activations, cond_scale, cond_shift, token_mask, shifted, sent):
    samples, rows, features = activations.shape
    diagonal = lax.broadcasted_iota(jnp.int32, (rows, rows), 0) == lax.broadcasted_iota(
        jnp.int32, (rows, rows), 1
    )
    for s in range(samples):
        normed = layer_norm(activations[s].astype(jnp.float32))
        result = cond_scale[s].astype(jnp.float32) * normed + cond_shift[s].astype(jnp.float32)
        flags = jnp.where(diagonal, token_mask[s : s + 1, :].astype(jnp.float32), 0.0)
        valid = jnp.sum(flags, axis=1, keepdims=True) > 0.0
        shifted[s] = result.astype(jnp.bfloat16)
        sent[s] = jnp.where(valid, result, absent).astype(jnp.bfloat16)


def attend_kernel(noise_size, heads, *refs):
    (mine, other, weights_mine, weights_other, query_bias, shifted, activations, output_gate) = refs[:8]
    bias_parts = refs[8 : 8 + noise_size]
    updated, full_weights, full_output, full_bias, keys, values, spread = refs[8 + noise_size :]
    groups, _, rows, features = mine.shape
    head_features = query_bias.shape[1]
    width = head_features // heads
    tokens = keys.shape[0]
    core = lax.rem(lax.axis_index("row"), 2)
    place = lax.axis_index("noise")
    lane = lax.broadcasted_iota(jnp.int32, (1, head_features), 1)

    @pl.when(pl.program_id(0) == 0)
    def _():
        depth, breadth = weights_mine.shape[2:]
        out_rows = depth // 2

        def take(of_keys, of_queries):
            for k in range(noise_size):
                block = place ^ k
                down = pl.ds(pl.multiple_of(block * depth, math.gcd(depth, 64)), depth)
                full_weights[down, 0:breadth] = of_queries[k, 0]
                full_weights[down, breadth : 2 * breadth] = of_keys[k, 0]
                full_weights[down, 2 * breadth : 3 * breadth] = of_keys[k, 1]
                across = pl.ds(pl.multiple_of(block * out_rows, math.gcd(out_rows, 32)), out_rows)
                halves = of_queries[k, 1].astype(full_output.dtype)
                full_output[across, 0:breadth] = halves[0:out_rows]
                full_output[across, breadth : 2 * breadth] = halves[out_rows:depth]

        @pl.when(core == 0)
        def _():
            take(weights_mine, weights_other)

        @pl.when(core != 0)
        def _():
            take(weights_other, weights_mine)

        for k in range(noise_size):
            part = bias_parts[k]
            columns = part.shape[2]
            along = pl.ds(pl.multiple_of((place ^ k) * columns, 128), columns)
            full_bias[:, along] = part[...].reshape(heads * rows, columns).astype(jnp.float32) * log2_e

    for source, parity in ((mine, core), (other, 1 - core)):
        block = source[...].reshape(groups * rows, features)
        projected = jnp.dot(
            block, full_weights[:, head_features:], preferred_element_type=jnp.float32
        ).astype(jnp.bfloat16)
        penalty = jnp.where(block[:, 0:1].astype(jnp.float32) > absent / 2, masked_score, 0.0)
        penalty = jnp.broadcast_to(penalty, (groups * rows, 128)).astype(jnp.bfloat16)
        for g in range(groups):
            here = slice(g * rows, (g + 1) * rows)
            down = pl.ds(pl.multiple_of((2 * g + parity) * rows, rows), rows)
            keys[down, 0:head_features] = projected[here, 0:head_features]
            keys[down, head_features:] = penalty[here]
            values[down, :] = projected[here, head_features:]

    queries = (
        jnp.dot(shifted[0], full_weights[:, 0:head_features], preferred_element_type=jnp.float32)
        + query_bias[...].astype(jnp.float32)
    ).astype(jnp.bfloat16)
    one = (lax.broadcasted_iota(jnp.int32, (rows, 128), 1) == 0).astype(jnp.bfloat16)
    for h in range(heads):
        inside = ((lane >= h * width) & (lane < (h + 1) * width)).astype(jnp.bfloat16)
        spread[h * rows : (h + 1) * rows, 0:head_features] = queries * inside
        spread[h * rows : (h + 1) * rows, head_features:] = one
    scores = lax.dot_general(
        spread[...], keys[...], (((1,), (1,)), ((), ())), preferred_element_type=jnp.float32
    )
    scores = scores * (log2_e / math.sqrt(width)) + full_bias[...]
    probs = jnp.exp2(scores - jnp.max(scores, axis=1, keepdims=True))
    total = jnp.sum(probs, axis=1, keepdims=True)
    mixture = jnp.dot(probs.astype(jnp.bfloat16), values[...], preferred_element_type=jnp.float32) / total
    attended = jnp.zeros((rows, head_features), jnp.float32)
    for h in range(heads):
        inside = (lane >= h * width) & (lane < (h + 1) * width)
        attended = jnp.where(inside, mixture[h * rows : (h + 1) * rows], attended)
    projected = jnp.dot(
        attended.astype(jnp.bfloat16), full_output[...].astype(jnp.bfloat16), preferred_element_type=jnp.float32
    )
    gate = jax.nn.sigmoid(output_gate[0].astype(jnp.float32))
    updated[0] = (activations[0].astype(jnp.float32) + gate * projected).astype(jnp.bfloat16)


def swap_cores(array):
    return lax.ppermute(array, "row", [(i, i ^ 1) for i in range(lax.axis_size("row"))])


def from_noise(array, k):
    if k == 0:
        return array
    return lax.ppermute(array, "noise", [(i, i ^ k) for i in range(lax.axis_size("noise"))])


def body(
    activations,
    cond_scale,
    cond_shift,
    output_gate,
    pair_repr,
    bias_weight,
    query_weight,
    query_bias,
    key_weight,
    value_weight,
    output_weight,
    token_mask,
):
    samples, rows, features = activations.shape
    heads = bias_weight.shape[1]
    head_features = query_weight.shape[1]
    row_size, noise_size = lax.axis_size("row"), lax.axis_size("noise")
    tokens = rows * row_size
    groups = row_size // 2
    core = lax.rem(lax.axis_index("row"), 2)

    shifted, sent = pl.pallas_call(
        shift_kernel,
        out_shape=[jax.ShapeDtypeStruct(activations.shape, jnp.bfloat16)] * 2,
        name="shift",
    )(activations, cond_scale, cond_shift, token_mask)
    mine = lax.all_gather(
        sent,
        "row",
        axis=0,
        axis_index_groups=[list(range(c, row_size, 2)) for c in range(2)],
    )
    other = swap_cores(mine)

    first = jnp.where(core == 0, key_weight, query_weight)
    output_halves = jnp.concatenate(
        [output_weight[:, :head_features], output_weight[:, head_features:]], axis=0
    )
    second = jnp.where(core == 0, value_weight, output_halves)
    half = jnp.stack([first, second])
    weights_mine = jnp.stack([from_noise(half, k) for k in range(noise_size)])
    weights_other = swap_cores(weights_mine)

    pair_normed = layer_norm(pair_repr.astype(jnp.float32))
    bias_tile = jnp.einsum(
        "ijc,ch->hij", pair_normed, bias_weight.astype(jnp.float32), precision=lax.Precision.HIGHEST
    ).astype(jnp.bfloat16)
    bias_parts = [from_noise(bias_tile, k) for k in range(noise_size)]

    whole = lambda array: pl.BlockSpec(array.shape, lambda s: (0,) * array.ndim)
    per_sample = pl.BlockSpec((1, rows, features), lambda s: (s, 0, 0))
    gathered = pl.BlockSpec((groups, 1, rows, features), lambda s: (0, s, 0, 0))
    bias_row = query_bias.reshape(1, head_features)
    padded = head_features + 128
    output_type = jnp.float32 if output_weight.shape[0] % 16 else jnp.bfloat16
    return pl.pallas_call(
        functools.partial(attend_kernel, noise_size, heads),
        grid=(samples,),
        in_specs=[
            gathered,
            gathered,
            whole(weights_mine),
            whole(weights_other),
            whole(bias_row),
            per_sample,
            per_sample,
            per_sample,
        ]
        + [whole(bias_tile)] * noise_size,
        out_specs=per_sample,
        out_shape=jax.ShapeDtypeStruct(activations.shape, jnp.bfloat16),
        scratch_shapes=[
            pltpu.VMEM((features, 3 * head_features), jnp.bfloat16),
            pltpu.VMEM((head_features, features), output_type),
            pltpu.VMEM((heads * rows, tokens), jnp.float32),
            pltpu.VMEM((tokens, padded), jnp.bfloat16),
            pltpu.VMEM((tokens, head_features), jnp.bfloat16),
            pltpu.VMEM((heads * rows, padded), jnp.bfloat16),
        ],
        compiler_params=pltpu.CompilerParams(vmem_limit_bytes=56 * 2**20),
        name="attend",
    )(
        mine,
        other,
        weights_mine,
        weights_other,
        bias_row,
        shifted,
        activations,
        output_gate,
        *bias_parts,
    )


def solution(mesh):
    return jax.shard_map(
        body,
        mesh=mesh,
        in_specs=(
            P("noise", "row", None),
            P("noise", "row", None),
            P("noise", "row", None),
            P("noise", "row", None),
            P("row", "noise", None),
            P(),
            P("noise", None),
            P(),
            P("noise", None),
            P("noise", None),
            P("noise", None),
            P("noise", "row"),
        ),
        out_specs=P("noise", "row", None),
        check_vma=False,
    )
```

time: 107 us -> 85.5 us (0.80)
  blocking collectives: 65.9 us -> 0 us
  waiting for transfers between devices: 0.06 us -> 37.7 us
  Pallas kernels: 0 us -> 13.1 us
  starting transfers between devices: 0.04 us -> 8.58 us
  matrix products: 12.5 us -> 4.01 us
  other arithmetic: 8.57 us -> 5.19 us
  local copies, waits for them, and re-layouts: 6.11 us -> 3.2 us
    all_gather x6 -> x0, blocking collectives: 65.9 us -> none  [the longest x1 12.3 us: body(): lax.all_gather(key_weight, 'noise', axis=0, tiled=True)]
    all_gather x2 -> x1, waiting for transfers between devices: 0.02 us -> 32.5 us  [body(): lax.all_gather(sent, 'row', axis=0, axis_index_groups=[list(range(c, row_...]
    pallas_call x0 -> x2, Pallas kernels: none -> 13.1 us  [the longest x1 10.6 us: body(): pl.pallas_call(functools.partial(attend_kernel, noise_size, heads), grid=...]
    ppermute x0 -> x8, starting transfers between devices: none -> 8.58 us  [the longest x6 8.01 us: from_noise(): lax.ppermute(array, 'noise', [(i, i ^ k) for i in range(lax.axis_size('no...]
    dot_general x6 -> x0, matrix products: 8.49 us -> none  [the longest x1 3.88 us: body(): jnp.einsum('shij,sjhd->shid', weights.astype(jnp.bfloat16), value_heads,...]
    ppermute x0 -> x8, waiting for transfers between devices: none -> 5.09 us  [the longest x6 5.09 us: from_noise(): lax.ppermute(array, 'noise', [(i, i ^ k) for i in range(lax.axis_size('no...]
    all_gather x2 -> x0, local copies, waits for them, and re-layouts: 3.43 us -> none  [the longest x1 1.72 us: body(): value_piece = lax.all_gather(value_rows, 'row', axis=1, tiled=True)]
    another operation x1 -> x3, other arithmetic: 0.01 us -> 2.16 us  [the longest x1 1.22 us: body(): half = jnp.stack([first, second])]
  transfers between devices with their start and end apart: 2 -> 9, of which waited for: 0 -> 3; matrix products, arithmetic and copies ran while one was open for 12% -> 13% of each run, Pallas kernels for 0% -> 0%
where the time goes in v1:
time: 85.5 us; the launch traced here: 85.3 us
  waiting for transfers between devices  37.7 us (44%)
  between operations  13.5 us (16%)
  Pallas kernels  13.1 us (15%)
  starting transfers between devices  8.58 us (10%)
  other arithmetic  5.19 us (6%)
  matrix products  4.01 us (5%)
  local copies, waits for them, and re-layouts  3.2 us (4%)
    all_gather x1, waiting for transfers between devices, body(): lax.all_gather(sent, 'row', axis=0, axis_index_groups=[list(range(c, row_...  32.5 us
    pallas_call x1, Pallas kernels, body(): pl.pallas_call(functools.partial(attend_kernel, noise_size, heads), grid=...  10.6 us
    ppermute x6, starting transfers between devices, from_noise(): lax.ppermute(array, 'noise', [(i, i ^ k) for i in range(lax.axis_size('no...  8.01 us
    ppermute x6, waiting for transfers between devices, from_noise(): lax.ppermute(array, 'noise', [(i, i ^ k) for i in range(lax.axis_size('no...  5.09 us
    dot_general x1, matrix products, body(): jnp.einsum('ijc,ch->hij', pair_normed, bias_weight.astype(jnp.float32), p...  4.01 us
    pallas_call x1, Pallas kernels, body(): pl.pallas_call(shift_kernel, out_shape=[jax.ShapeDtypeStruct(activations....  2.53 us
    reduce_sum x1, other arithmetic, layer_norm(): variance = jnp.mean(centred * centred, axis=-1, keepdims=True)  2.39 us
  transfers between devices with their start and end apart: 9, of which 3 were waited for; matrix products, arithmetic and copies ran while one was open for 13% of the time, Pallas kernels for 0%

profile of v1, /device:TPU:0, one launch (start us, length us, event | category | flops | bytes accessed | tf_op | source)
XLA Modules:
  0.0 85.3 jit_solution(4971719258994222431)
XLA Ops:
  6.5 0.0 copy-start
  6.5 0.0 all-gather.3.cloned.1.call-start
  6.5 2.5 %shift.1 = (bf16[4,64,768]{2,1,0:T(8,128)(2,1)}, bf16[4,64,768]{2,1,0:T(8,128)(2,1)}) custom-call(bf16[4,64,768]{2,1,0:T(8,128)(2,1)} %refs_6_.1, bf16[4,64,768]{2,1,0:T(8,128)(2,1)} %cond_scale.1, bf16[4,64,768]{2,1,0:T(8,128)(2,1)} %cond_shift.1, s32[4,64]{1,0:T(4,128)} %token_mask.1), custom_call_target="tpu_custom_call" | custom-call | tf_op jit(solution)/shard_map/shift/pallas_call | solution.py:154
  9.1 0.0 all-gather.3.cloned.1.call-update
  9.1 0.9 %fusion.11 = (bf16[96,384]{1,0:T(8,128)(2,1)S(1)}, bf16[96,384]{1,0:T(8,128)(2,1)S(1)}) fusion(bf16[96,768]{1,0:T(8,128)(2,1)} %param.22), kind=kLoop, calls=%fused_computation.19 | loop fusion | bytes 294912 | tf_op jit(solution)/shard_map/slice | solution.py:169
  10.0 0.0 copy-start.1
  10.1 1.2 %fusion.7 = (bf16[1,192,384]{2,1,0:T(8,128)(2,1)S(1)}, bf16[1,192,384]{2,1,0:T(8,128)(2,1)S(1)}) fusion(bf16[192,384]{1,0:T(8,128)(2,1)} %param.21, bf16[96,384]{1,0:T(8,128)(2,1)S(1)} %get-tuple-element.12, bf16[96,384]{1,0:T(8,128)(2,1)S(1)} %get-tuple-element.11, pred[]{:T(512)S(6)} %eq.4, bf16[192,384]{1,0:T(8,128)(2,1)} %param.20, ...), kind=kLoop, calls=%fused_computation.12 | loop fusion | flops 442368 | bytes 884737 | tf_op jit(solution)/shard_map/stack | solution.py:172
  11.3 0.8 fusion.10
  12.0 3.0 %collective-permute-start.2 = (bf16[2,192,384]{2,1,0:T(8,128)(2,1)}, bf16[2,192,384]{2,1,0:T(8,128)(2,1)S(1)}, u32[]{:S(2)}, u32[]{:S(2)}) collective-permute-start(bf16[2,192,384]{2,1,0:T(8,128)(2,1)} %get-tuple-element.10), channel_id=1, source_target_pairs={{0,16},{8,24},{16,0},{24,8},{1,17},{9,25},{17,1},{25,9},{2,18},{10... | collective-permute-start | bytes 884744 | tf_op jit(solution)/shard_map/ppermute | solution.py:129
  15.0 1.5 %collective-permute-start.1 = (bf16[2,192,384]{2,1,0:T(8,128)(2,1)}, bf16[2,192,384]{2,1,0:T(8,128)(2,1)S(1)}, u32[]{:S(2)}, u32[]{:S(2)}) collective-permute-start(bf16[2,192,384]{2,1,0:T(8,128)(2,1)} %get-tuple-element.10), channel_id=1, source_target_pairs={{0,8},{8,0},{16,24},{24,16},{1,9},{9,1},{17,25},{25,17},{2,10},{10... | collective-permute-start | bytes 884744 | tf_op jit(solution)/shard_map/ppermute | solution.py:129
  16.5 0.0 collective-permute-start.3
  16.5 32.5 %all-gather.3.cloned.1.call-done = bf16[16,64,768]{2,1,0:T(8,128)(2,1)} async-done(((bf16[4,64,768]{2,1,0:T(8,128)(2,1)}), bf16[16,64,768]{2,1,0:T(8,128)(2,1)}) %all-gather.3.cloned.1.call-update) | async-done | bytes 1572880 | tf_op jit(solution)/shard_map/all_gather | solution.py:159
  49.0 0.0 collective-permute-start
  49.0 0.0 collective-permute-done.2
  49.0 0.0 collective-permute-done.1
  49.1 0.0 collective-permute-done.3
  49.1 0.2 pad_maximum_fusion.refs_2_
  49.3 0.0 copy-start.2
  49.3 0.6 collective-permute-start.4
  49.8 0.0 copy-done.1
  49.8 0.6 convert_reduce_fusion
  50.5 2.4 %fusion.2 = f32[64,128]{1,0:T(8,128)S(1)} fusion(bf16[64,128,128]{2,1,0:T(8,128)(2,1)S(1)} %copy-done.1, f32[64,128]{1,0:T(8,128)S(1)} %broadcast_multiply_fusion), kind=kLoop, calls=%fused_computation.4 | loop fusion | flops 4186112 | bytes 2162688 | tf_op jit(solution)/shard_map/reduce_sum | solution.py:20
  52.9 0.0 copy-done.2
  52.9 0.0 copy-start.9
  52.9 0.0 copy-done
  52.9 4.0 %fusion.3 = bf16[64,128,8]{1,2,0:T(8,128)(2,1)S(1)} fusion(bf16[64,128,128]{2,1,0:T(8,128)(2,1)S(1)} %copy-done.1, f32[64,128]{1,0:T(8,128)S(1)} %add_rsqrt_fusion, f32[64,128]{1,0:T(8,128)S(1)} %broadcast_multiply_fusion, bf16[128,8]{0,1:T(8,128)(2,1)S(1)} %copy-done), kind=kOutput, calls=%fused_computation.5 | convolution fusion | flops 103809024 | bytes 2295808 | tf_op jit(solution)/shard_map/ijc,ch->hij/dot_general | solution.py:177
  57.0 0.0 copy-start.5
  57.0 2.4 %collective-permute-start.7 = (bf16[8,64,128]{2,1,0:T(8,128)(2,1)S(1)}, bf16[8,64,128]{2,1,0:T(8,128)(2,1)S(1)}, u32[]{:S(2)}, u32[]{:S(2)}) collective-permute-start(bf16[8,64,128]{2,1,0:T(8,128)(2,1)S(1)} %bitcast.18), channel_id=1, source_target_pairs={{0,24},{8,16},{16,8},{24,0},{1,25},{9,17},{17,9},{25,1},{2,26},{10... | collective-permute-start | bytes 393224 | tf_op jit(solution)/shard_map/ppermute | solution.py:129
  59.4 0.6 collective-permute-start.6
  60.0 0.6 collective-permute-start.5
  60.5 0.0 copy-done.9
  60.5 0.6 reshape.15.refs_4_
  61.1 2.6 %collective-permute-done.7.refs_11_ = bf16[8,64,128]{2,1,0:T(8,128)(2,1)S(1)} collective-permute-done((bf16[8,64,128]{2,1,0:T(8,128)(2,1)S(1)}, bf16[8,64,128]{2,1,0:T(8,128)(2,1)S(1)}, u32[]{:S(2)}, u32[]{:S(2)}) %collective-permute-start.7) | collective-permute-done | bytes 131104 | tf_op jit(solution)/shard_map/ppermute | solution.py:129
  63.7 0.0 copy-start.6
  63.7 2.4 %collective-permute-done.6.refs_10_ = bf16[8,64,128]{2,1,0:T(8,128)(2,1)S(1)} collective-permute-done((bf16[8,64,128]{2,1,0:T(8,128)(2,1)S(1)}, bf16[8,64,128]{2,1,0:T(8,128)(2,1)S(1)}, u32[]{:S(2)}, u32[]{:S(2)}) %collective-permute-start.6) | collective-permute-done | bytes 131104 | tf_op jit(solution)/shard_map/ppermute | solution.py:129
  66.2 0.0 copy-start.7
  66.2 0.0 collective-permute-done.5.refs_9_
  66.2 0.0 copy-start.8
  66.2 0.0 collective-permute-done.4.refs_3_
  66.2 0.0 copy-start.4
  66.2 0.0 collective-permute-done.refs_1_
  66.2 0.0 copy-start.3
  66.2 0.0 copy-done.5
  66.2 0.0 copy-done.6
  66.2 0.6 copy-done.7
  66.8 0.1 copy-done.8
  66.9 0.4 copy-done.4
  67.3 0.5 copy-done.3
  67.9 10.6 %attend.1 = bf16[4,64,768]{2,1,0:T(8,128)(2,1)} custom-call(bf16[4,4,64,768]{3,2,1,0:T(8,128)(2,1)} %bitcast.17, bf16[4,4,64,768]{3,2,1,0:T(8,128)(2,1)} %copy-done.3, bf16[4,2,192,384]{3,2,1,0:T(8,128)(2,1)} %copy-done.2, bf16[4,2,192,384]{3,2,1,0:T(8,128)(2,1)} %copy-done.4, bf16[1,384]{1,0:T(2,128)(2,1)} %reshape.15.refs_4_, ...), custom_call_target="tpu_custom_call" | custom-call | tf_op jit(solution)/shard_map/attend/pallas_call | solution.py:188
  (3 shorter events, 0.0 us)
Async XLA Ops:
  6.5 46.4 %copy-start = (bf16[128,8]{0,1:T(8,128)(2,1)S(1)}, bf16[128,8]{0,1:T(8,128)(2,1)}, u32[]{:S(2)}) copy-start(bf16[128,8]{0,1:T(8,128)(2,1)} %param.17) | copy-start | bytes 6148
  6.5 42.5 %all-gather.3.cloned.1.call-start = ((), (), s32[]{:S(2)}) async-start(), calls=%async_computation | async-start | bytes 1966080 | tf_op jit(solution)/shard_map/all_gather | solution.py:159
  10.0 39.8 %copy-start.1 = (bf16[64,128,128]{2,1,0:T(8,128)(2,1)S(1)}, bf16[64,128,128]{2,1,0:T(8,128)(2,1)}, u32[]{:S(2)}) copy-start(bf16[64,128,128]{2,1,0:T(8,128)(2,1)} %param.16) | copy-start | bytes 6291460
  12.0 37.0 %collective-permute-start.2 = (bf16[2,192,384]{2,1,0:T(8,128)(2,1)}, bf16[2,192,384]{2,1,0:T(8,128)(2,1)S(1)}, u32[]{:S(2)}, u32[]{:S(2)}) collective-permute-start(bf16[2,192,384]{2,1,0:T(8,128)(2,1)} %get-tuple-element.10), channel_id=1, source_target_pairs={{0,16},{8,24},{16,0},{24,8},{1,17},{9,25},{17,1},{25,9},{2,18},{10... | collective-permute-start | bytes 884744 | tf_op jit(solution)/shard_map/ppermute | solution.py:129
  15.0 34.1 %collective-permute-start.1 = (bf16[2,192,384]{2,1,0:T(8,128)(2,1)}, bf16[2,192,384]{2,1,0:T(8,128)(2,1)S(1)}, u32[]{:S(2)}, u32[]{:S(2)}) collective-permute-start(bf16[2,192,384]{2,1,0:T(8,128)(2,1)} %get-tuple-element.10), channel_id=1, source_target_pairs={{0,8},{8,0},{16,24},{24,16},{1,9},{9,1},{17,25},{25,17},{2,10},{10... | collective-permute-start | bytes 884744 | tf_op jit(solution)/shard_map/ppermute | solution.py:129
  16.5 32.6 %collective-permute-start.3 = (bf16[2,192,384]{2,1,0:T(8,128)(2,1)}, bf16[2,192,384]{2,1,0:T(8,128)(2,1)S(1)}, u32[]{:S(2)}, u32[]{:S(2)}) collective-permute-start(bf16[2,192,384]{2,1,0:T(8,128)(2,1)} %get-tuple-element.10), channel_id=1, source_target_pairs={{0,24},{8,16},{16,8},{24,0},{1,25},{9,17},{17,9},{25,1},{2,26},{10... | collective-permute-start | bytes 884744 | tf_op jit(solution)/shard_map/ppermute | solution.py:129
  49.0 17.2 %collective-permute-start = (bf16[4,4,64,768]{3,2,1,0:T(8,128)(2,1)}, bf16[4,4,64,768]{3,2,1,0:T(8,128)(2,1)S(1)}, u32[]{:S(2)}, u32[]{:S(2)}) collective-permute-start(bf16[4,4,64,768]{3,2,1,0:T(8,128)(2,1)} %bitcast.16), channel_id=1, source_target_pairs={{0,1},{1,0},{2,3},{3,2},{4,5},{5,4},{6,7},{7,6},{8,9},{9,8},{10,11... | collective-permute-start | bytes 4718600 | tf_op jit(solution)/shard_map/ppermute | solution.py:123
  49.3 3.6 %copy-start.2 = (bf16[4,2,192,384]{3,2,1,0:T(8,128)(2,1)}, bf16[4,2,192,384]{3,2,1,0:T(8,128)(2,1)S(1)}, u32[]{:S(2)}) copy-start(bf16[4,2,192,384]{3,2,1,0:T(8,128)(2,1)S(1)} %pad_maximum_fusion.refs_2_) | copy-start | bytes 3538948
  49.3 16.9 %collective-permute-start.4 = (bf16[4,2,192,384]{3,2,1,0:T(8,128)(2,1)S(1)}, bf16[4,2,192,384]{3,2,1,0:T(8,128)(2,1)S(1)}, u32[]{:S(2)}, u32[]{:S(2)}) collective-permute-start(bf16[4,2,192,384]{3,2,1,0:T(8,128)(2,1)S(1)} %pad_maximum_fusion.refs_2_), channel_id=1, source_target_pairs={{0,1},{1,0},{2,3},{3,2},{4,5},{5,4},{6,7},{7,6},{8,9},{9,8},{10,11... | collective-permute-start | bytes 3538952 | tf_op jit(solution)/shard_map/ppermute | solution.py:123
  52.9 7.7 %copy-start.9 = (bf16[384]{0:T(512)(128)(2,1)S(1)}, bf16[384]{0:T(512)(128)(2,1)}, u32[]{:S(2)}) copy-start(bf16[384]{0:T(512)(128)(2,1)} %param.19) | copy-start | bytes 2308
  57.0 9.3 %copy-start.5 = (bf16[64,128,8]{1,0,2:T(8,128)(2,1)}, bf16[64,128,8]{1,0,2:T(8,128)(2,1)S(1)}, u32[]{:S(2)}) copy-start(bf16[64,128,8]{1,0,2:T(8,128)(2,1)S(1)} %copy.18) | copy-start | bytes 393220
  57.0 6.8 %collective-permute-start.7 = (bf16[8,64,128]{2,1,0:T(8,128)(2,1)S(1)}, bf16[8,64,128]{2,1,0:T(8,128)(2,1)S(1)}, u32[]{:S(2)}, u32[]{:S(2)}) collective-permute-start(bf16[8,64,128]{2,1,0:T(8,128)(2,1)S(1)} %bitcast.18), channel_id=1, source_target_pairs={{0,24},{8,16},{16,8},{24,0},{1,25},{9,17},{17,9},{25,1},{2,26},{10... | collective-permute-start | bytes 393224 | tf_op jit(solution)/shard_map/ppermute | solution.py:129
  59.4 6.8 %collective-permute-start.6 = (bf16[8,64,128]{2,1,0:T(8,128)(2,1)S(1)}, bf16[8,64,128]{2,1,0:T(8,128)(2,1)S(1)}, u32[]{:S(2)}, u32[]{:S(2)}) collective-permute-start(bf16[8,64,128]{2,1,0:T(8,128)(2,1)S(1)} %bitcast.19), channel_id=1, source_target_pairs={{0,16},{8,24},{16,0},{24,8},{1,17},{9,25},{17,1},{25,9},{2,18},{10... | collective-permute-start | bytes 393224 | tf_op jit(solution)/shard_map/ppermute | solution.py:129
  60.0 6.2 %collective-permute-start.5 = (bf16[8,64,128]{2,1,0:T(8,128)(2,1)S(1)}, bf16[8,64,128]{2,1,0:T(8,128)(2,1)S(1)}, u32[]{:S(2)}, u32[]{:S(2)}) collective-permute-start(bf16[8,64,128]{2,1,0:T(8,128)(2,1)S(1)} %bitcast.20), channel_id=1, source_target_pairs={{0,8},{8,0},{16,24},{24,16},{1,9},{9,1},{17,25},{25,17},{2,10},{10... | collective-permute-start | bytes 393224 | tf_op jit(solution)/shard_map/ppermute | solution.py:129
  63.7 2.5 %copy-start.6 = (bf16[8,64,128]{2,1,0:T(8,128)(2,1)}, bf16[8,64,128]{2,1,0:T(8,128)(2,1)S(1)}, u32[]{:S(2)}) copy-start(bf16[8,64,128]{2,1,0:T(8,128)(2,1)S(1)} %collective-permute-done.7.refs_11_) | copy-start | bytes 393220
  66.2 0.6 copy-start.7
  66.2 0.7 copy-start.8
  66.2 1.1 %copy-start.4 = (bf16[4,2,192,384]{3,2,1,0:T(8,128)(2,1)}, bf16[4,2,192,384]{3,2,1,0:T(8,128)(2,1)S(1)}, u32[]{:S(2)}) copy-start(bf16[4,2,192,384]{3,2,1,0:T(8,128)(2,1)S(1)} %collective-permute-done.4.refs_3_) | copy-start | bytes 3538948
  66.2 1.7 %copy-start.3 = (bf16[4,4,64,768]{3,2,1,0:T(8,128)(2,1)}, bf16[4,4,64,768]{3,2,1,0:T(8,128)(2,1)S(1)}, u32[]{:S(2)}) copy-start(bf16[4,4,64,768]{3,2,1,0:T(8,128)(2,1)S(1)} %collective-permute-done.refs_1_) | copy-start | bytes 4718596
Sparse Core Ops, SparseCore 0:
  9.2 39.7 all-gather.2
